TPU v7x, 32 devices: a whole 2x2x4 slice. The times are simulated.
32 devices in a mesh: req: 8 (over z, y), grp: 4 (over x, core).
Axes of the slice: x: 2, y: 2, z: 4, core: 2. Of those that a mesh axis runs over, the one named last changes fastest.
Arguments:
- hidden: bfloat16 [8192, 1536], P(('req', 'grp')), may hold values from -48 to 48
- queries: bfloat16 [8192, 1536], P(('req', 'grp')), may hold values from -8 to 8
- new_cache: bfloat16 [8192, 256], P(('req', 'grp')), may hold values from -8 to 8
- cache_pool: bfloat16 [8192, 64, 256], P(('req', 'grp')), may hold values from -6 to 6
- cache_length: int32 [128], P(('req', 'grp')), may hold values from 1 to 4096
- page_table: int32 [128, 17], P(('req', 'grp')), may hold values from 0 to 95, as said below
- send_map: int32 [32, 96], P(('req', 'grp')), may hold values from 0 to 255, as said below
- out_weight: bfloat16 [1536, 1536], replicated, may hold values from -0.5 to 0.5
- norm_gain: bfloat16 [1536], replicated, may hold values from 0.099609375 to 1.8984375
- ffn_weight: bfloat16 [3, 1536, 4608], P(None, None, 'grp'), may hold values from -0.15625 to 0.15625
Outputs:
- block_out: bfloat16 [8192, 1536], P(('req', 'grp'))
Inputs may be any that keep to these rules, and one draw needn't show every extreme that they name: `page_table`: the 68 entries of one device's requests are distinct; entry s * 3 + c names the page that device s sends to that device as its slot c. On every device all 3 slots of some source are named. `send_map`: entry d * 3 + c of row s is the slot of device s's pool that it sends to device d as slot c; the entries of a row are distinct.
All inputs are finite; a program needn't handle non-finite values.
Results may differ from a plain program's by a relative error of at most 0.012.
Values may be sent and summed in bfloat16 or wider, within the bound.
A program may use at most 128 MiB of HBM per device.

v0:
```python
import math

import jax
import jax.numpy as jnp
from jax import lax
from jax.sharding import PartitionSpec as P

W = 1024
PAGE = 64


masked_score = -1e30


def visibility(lengths, first_page, page_size, window, new_count, cache_slots):
    query_pos = lengths[:, None] + jnp.arange(new_count, dtype=jnp.int32)[None, :]
    cache_pos = first_page[:, None] * page_size + jnp.arange(cache_slots, dtype=jnp.int32)[None, :]
    cache_seen = (cache_pos[:, None, :] < lengths[:, None, None]) & (
        cache_pos[:, None, :] > query_pos[:, :, None] - window
    )
    offsets = jnp.arange(new_count, dtype=jnp.int32)
    fresh_seen = offsets[None, None, :] <= offsets[None, :, None]
    fresh_seen = jnp.broadcast_to(fresh_seen, (lengths.shape[0], new_count, new_count))
    return jnp.concatenate([cache_seen, fresh_seen], axis=2)


def normalize(scores, seen):
    scores = jnp.where(seen[:, None], scores, masked_score)
    top_score = jnp.max(scores, axis=-1, keepdims=True)
    weights = jnp.where(seen[:, None], jnp.exp(scores - top_score), 0.0)
    return (weights / jnp.sum(weights, axis=-1, keepdims=True)).astype(jnp.bfloat16)


def expand_rows(rows, weight_block):
    gate_part = jnp.dot(rows, weight_block[0], preferred_element_type=jnp.float32)
    up_part = jnp.dot(rows, weight_block[1], preferred_element_type=jnp.float32)
    return (jax.nn.gelu(gate_part, approximate=True) * up_part).astype(jnp.bfloat16)


def contract_rows(activated, weight_block):
    return lax.dot_general(
        activated, weight_block[2], (((1,), (1,)), ((), ())), preferred_element_type=jnp.float32
    )


def per_device(
    hidden,
    queries,
    new_cache,
    cache_pool,
    cache_length,
    page_table,
    send_map,
    out_weight,
    norm_gain,
    ffn_weight,
):
    page_size = cache_pool.shape[1]
    pair_width = cache_pool.shape[2]
    head_size = pair_width // 2
    requests = cache_length.shape[0]
    wpages = page_table.shape[1]
    tok_rows = queries.shape[0]
    new_count = tok_rows // requests
    head_count = queries.shape[1] // head_size
    outgoing = cache_pool[send_map[0]]
    arrived = lax.all_to_all(outgoing, ("req", "grp"), split_axis=0, concat_axis=0, tiled=True)
    cache_slots = wpages * page_size
    window_rows = arrived[page_table].reshape(requests, cache_slots, pair_width)
    both = jnp.concatenate(
        [window_rows, new_cache.reshape(requests, new_count, pair_width)], axis=1
    )
    key_rows = both[:, :, :head_size]
    value_rows = both[:, :, head_size:]
    first_page = jnp.maximum(cache_length - W + 1, 0) // PAGE
    seen = visibility(cache_length, first_page, page_size, W, new_count, cache_slots)
    query_block = queries.reshape(requests, new_count, head_count, head_size)
    scores = jnp.einsum(
        "rnhe,rke->rhnk", query_block, key_rows, preferred_element_type=jnp.float32
    ) / math.sqrt(head_size)
    attn_probs = normalize(scores, seen)
    attended = jnp.einsum(
        "rhnk,rke->rnhe", attn_probs, value_rows, preferred_element_type=jnp.float32
    )
    attended = attended.astype(jnp.bfloat16).reshape(tok_rows, head_count * head_size)
    projected = jnp.dot(attended, out_weight, preferred_element_type=jnp.float32)
    middle = (hidden.astype(jnp.float32) + projected).astype(jnp.bfloat16)
    middle_f = middle.astype(jnp.float32)
    scale_rows = lax.rsqrt(jnp.mean(middle_f * middle_f, axis=-1, keepdims=True) + 1e-06)
    normed = (middle_f * scale_rows * norm_gain.astype(jnp.float32)).astype(jnp.bfloat16)
    activated_all = expand_rows(lax.all_gather(normed, "grp", axis=0, tiled=True), ffn_weight)
    ffn_sum = lax.psum_scatter(
        contract_rows(activated_all, ffn_weight), "grp", scatter_dimension=0, tiled=True
    )
    return (middle_f + ffn_sum).astype(jnp.bfloat16)


def solution(mesh):
    return jax.shard_map(
        per_device,
        mesh=mesh,
        in_specs=(
            P(("req", "grp"), None),
            P(("req", "grp"), None),
            P(("req", "grp"), None),
            P(("req", "grp"), None, None),
            P(("req", "grp")),
            P(("req", "grp"), None),
            P(("req", "grp"), None),
            P(),
            P(),
            P(None, None, "grp"),
        ),
        out_specs=P(("req", "grp"), None),
        check_vma=False,
    )
```

profile of v0, /device:TPU:0, one launch (start us, length us, event | category | flops | bytes accessed | tf_op | source)
XLA Modules:
  0.0 235.4 jit_solution(9660540738897386921)
XLA Ops:
  6.5 0.7 fusion.43
  7.2 5.9 %gather_fusion = bf16[96,64,256]{2,1,0:T(8,128)(2,1)} fusion(bf16[256,64,256]{2,1,0:T(8,128)(2,1)} %param.13, s32[1024]{0:T(1024)S(1)} %pad_clamp_fusion.1), kind=kCustom, calls=%fused_computation | custom fusion | bytes 6291840 | tf_op jit(solution)/shard_map/gather | solution.py:66
  13.1 7.3 %all-to-all-start = ((bf16[96,64,256]{2,1,0:T(8,128)(2,1)}), bf16[96,64,256]{2,1,0:T(8,128)(2,1)S(1)}, u32[]{:S(2)}, u32[]{:S(2)}) async-start(bf16[96,64,256]{2,1,0:T(8,128)(2,1)} %gather_fusion), calls=%async_computation | async-start | bytes 6291456 | tf_op jit(solution)/shard_map/all_to_all | solution.py:67
  20.4 0.0 all-gather.2.cloned.1.call-start
  20.5 0.0 copy-done.2
  20.5 0.1 reshape.150
  20.6 2.4 %reshape.138 = bf16[4,64,12,128]{3,2,1,0:T(8,128)(2,1)} reshape(bf16[256,1536]{1,0:T(8,128)(2,1)} %param.11) | data formatting | bytes 1572864 | tf_op jit(solution)/shard_map/reshape | solution.py:77
  23.0 0.0 copy-done.1
  23.0 0.0 copy-done.3
  23.0 0.1 add_add_fusion
  23.1 0.1 broadcast_compare_fusion
  23.2 0.1 iota_add_fusion
  23.3 0.3 compare_and_fusion
  23.6 0.1 pad_add_fusion
  23.7 68.2 %all-to-all-done = bf16[96,64,256]{2,1,0:T(8,128)(2,1)S(1)} async-done(((bf16[96,64,256]{2,1,0:T(8,128)(2,1)}), bf16[96,64,256]{2,1,0:T(8,128)(2,1)S(1)}, u32[]{:S(2)}, u32[]{:S(2)}) %all-to-all-start) | async-done | bytes 3145760 | tf_op jit(solution)/shard_map/all_to_all | solution.py:67
  91.9 2.3 gather_fusion.1
  94.2 10.5 %fusion.51 = (f32[4,12,64]{2,1,0:T(8,128)S(1)}, f32[4,12,64,1152]{3,2,1,0:T(8,128)}) fusion(pred[4,64,1152]{2,1,0:T(8,128)(4,1)S(1)} %pad_add_fusion, bf16[4,64,12,128]{3,2,1,0:T(8,128)(2,1)} %reshape.138, bf16[4,64,256]{2,1,0:T(8,128)(2,1)} %bitcast.52, bf16[4,1088,256]{2,1,0:T(8,128)(2,1)} %bitcast.49), kind=kOutput, calls=%fused_computation.68 | convolution fusion | flops 926024832 | bytes 17608704 | tf_op jit(solution)/shard_map/sub | solution.py:30
  104.6 0.0 copy-done
  104.6 7.1 %fusion.27 = bf16[4,64,12,128]{3,1,2,0:T(8,128)(2,1)S(1)} fusion(f32[4,12,64,1152]{3,2,1,0:T(8,128)} %get-tuple-element.6, f32[4,12,64]{2,1,0:T(8,128)S(1)} %get-tuple-element.5, bf16[4,1088,256]{2,1,0:T(8,128)(2,1)S(1)} %bitcast.50, bf16[4,64,256]{2,1,0:T(8,128)(2,1)S(1)} %bitcast.53), kind=kOutput, calls=%fused_computation.39 | convolution fusion | flops 915800064 | bytes 17313792 | tf_op jit(solution)/shard_map/rhnk,rke->rnhe/dot_general | solution.py:82
  111.8 0.5 copy.13
  112.3 3.8 %multiply_reduce_fusion = (f32[256]{0:T(256)S(1)}, f32[256,1536]{1,0:T(8,128)S(1)}) fusion(bf16[1536,1536]{1,0:T(8,128)(2,1)} %param.17, bf16[32,8,12,128]{3,2,1,0:T(8,128)(2,1)S(1)} %bitcast.51, bf16[256,1536]{1,0:T(8,128)(2,1)S(1)} %copy-done.5), kind=kOutput, calls=%fused_computation.37 | convolution fusion | flops 1210318592 | bytes 7865344 | tf_op jit(solution)/shard_map/dot_general | solution.py:86
  116.2 1.1 multiply_convert_fusion
  117.3 0.0 all-gather.2.cloned.1.call-update
  117.3 0.2 reduce-scatter.2.cloned.1.call-start
  117.5 27.8 %all-gather.2.cloned.1.call-done = bf16[1024,1536]{1,0:T(8,128)(2,1)} async-done(((bf16[256,1536]{1,0:T(8,128)(2,1)}), bf16[1024,1536]{1,0:T(8,128)(2,1)}) %all-gather.2.cloned.1.call-update) | async-done | bytes 3145744 | tf_op jit(solution)/shard_map/all_gather | solution.py:91
  145.3 7.3 %fusion.17 = f32[1024,1152]{1,0:T(8,128)S(1)} fusion(bf16[1024,1536]{1,0:T(8,128)(2,1)} %all-gather.2.cloned.1.call-done, bf16[3,1536,1152]{2,1,0:T(8,128)(2,1)} %param.19), kind=kOutput, calls=%fused_computation.24 | convolution fusion | flops 3623878656 | bytes 11403264 | tf_op jit(solution)/shard_map/dot_general | solution.py:35
  152.6 0.0 copy-done.4
  152.6 6.8 %fusion.13 = bf16[1024,1152]{1,0:T(8,128)(2,1)S(1)} fusion(bf16[1024,1536]{1,0:T(8,128)(2,1)S(1)} %copy-done.4, f32[1024,1152]{1,0:T(8,128)S(1)} %fusion.17, bf16[3,1536,1152]{2,1,0:T(8,128)(2,1)} %param.19), kind=kOutput, calls=%fused_computation.20 | convolution fusion | flops 3635675136 | bytes 13762560 | tf_op jit(solution)/shard_map/dot_general | solution.py:36
  159.4 8.2 %fusion.14 = f32[1024,1536]{1,0:T(8,128)} fusion(bf16[1024,1152]{1,0:T(8,128)(2,1)S(1)} %fusion.13, bf16[3,1536,1152]{2,1,0:T(8,128)(2,1)} %param.19), kind=kOutput, calls=%fused_computation.21 | convolution fusion | flops 3623878656 | bytes 12189696 | tf_op jit(solution)/shard_map/dot_general | solution.py:41
  167.6 0.0 reduce-scatter.2.cloned.1.call-update
  167.6 58.5 %reduce-scatter.2.cloned.1.call-done = f32[256,1536]{1,0:T(8,128)} async-done(((f32[1024,1536]{1,0:T(8,128)}), f32[256,1536]{1,0:T(8,128)}) %reduce-scatter.2.cloned.1.call-update) | async-done | bytes 1572880 | tf_op jit(solution)/shard_map/reduce_scatter | solution.py:92
  226.1 2.5 %add_convert_fusion = bf16[256,1536]{1,0:T(8,128)(2,1)} fusion(f32[256,1536]{1,0:T(8,128)S(1)} %get-tuple-element.8, f32[256,1536]{1,0:T(8,128)} %reduce-scatter.2.cloned.1.call-done), kind=kLoop, calls=%fused_computation.35 | loop fusion | flops 786432 | bytes 3932160 | tf_op jit(solution)/shard_map/convert_element_type | solution.py:95
  (17 shorter events, 0.1 us)
Async XLA Ops:
  13.1 7.4 %copy-start.2 = (s32[4,17]{1,0:T(4,128)S(1)}, s32[4,17]{1,0:T(4,128)}, u32[]{:S(2)}) copy-start(s32[4,17]{1,0:T(4,128)} %param.15) | copy-start | bytes 820
  13.1 9.9 %copy-start.1 = (bf16[1536]{0:T(1024)(128)(2,1)S(1)}, bf16[1536]{0:T(1024)(128)(2,1)}, u32[]{:S(2)}) copy-start(bf16[1536]{0:T(1024)(128)(2,1)} %param.18) | copy-start | bytes 9220
  13.1 9.9 %copy-start.3 = (s32[4]{0:T(128)S(1)}, s32[4]{0:T(128)}, u32[]{:S(2)}) copy-start(s32[4]{0:T(128)} %param.14) | copy-start | bytes 52
  13.1 78.8 %all-to-all-start = ((bf16[96,64,256]{2,1,0:T(8,128)(2,1)}), bf16[96,64,256]{2,1,0:T(8,128)(2,1)S(1)}, u32[]{:S(2)}, u32[]{:S(2)}) async-start(bf16[96,64,256]{2,1,0:T(8,128)(2,1)} %gather_fusion), calls=%async_computation | async-start | bytes 6291456 | tf_op jit(solution)/shard_map/all_to_all | solution.py:67
  20.4 124.9 %all-gather.2.cloned.1.call-start = ((), (), s32[]{:S(2)}) async-start(), calls=%async_computation.2 | async-start | bytes 3932160 | tf_op jit(solution)/shard_map/all_gather | solution.py:91
  94.2 10.5 %copy-start = (bf16[68,64,256]{2,1,0:T(8,128)(2,1)S(1)}, bf16[68,64,256]{2,1,0:T(8,128)(2,1)}, u32[]{:S(2)}) copy-start(bf16[68,64,256]{2,1,0:T(8,128)(2,1)} %gather_fusion.1) | copy-start | bytes 6684676
  94.2 10.5 %copy-start.6 = (bf16[256,256]{1,0:T(8,128)(2,1)S(1)}, bf16[256,256]{1,0:T(8,128)(2,1)}, u32[]{:S(2)}) copy-start(bf16[256,256]{1,0:T(8,128)(2,1)} %param.12) | copy-start | bytes 393220
  104.6 7.7 %copy-start.5 = (bf16[256,1536]{1,0:T(8,128)(2,1)S(1)}, bf16[256,1536]{1,0:T(8,128)(2,1)}, u32[]{:S(2)}) copy-start(bf16[256,1536]{1,0:T(8,128)(2,1)} %param.10) | copy-start | bytes 2359300
  117.3 108.9 %reduce-scatter.2.cloned.1.call-start = ((), (), s32[]{:S(2)}) async-start(), calls=%async_computation.3 | async-start | bytes 7864320 | tf_op jit(solution)/shard_map/reduce_scatter | solution.py:92
  145.3 7.3 %copy-start.4 = (bf16[1024,1536]{1,0:T(8,128)(2,1)S(1)}, bf16[1024,1536]{1,0:T(8,128)(2,1)}, u32[]{:S(2)}) copy-start(bf16[1024,1536]{1,0:T(8,128)(2,1)} %all-gather.2.cloned.1.call-done) | copy-start | bytes 9437188
Sparse Core Ops, SparseCore 0:
  117.4 27.8 all-gather.1
  167.7 58.3 reduce-scatter.1
where the time goes:
time: 236 us; the launch traced here: 235 us
  waiting for transfers between devices  155 us (66%)
  matrix products  43.7 us (19%)
  between operations  13.5 us (6%)
  local copies, waits for them, and re-layouts  11.2 us (5%)
  starting transfers between devices  7.56 us (3%)
  other arithmetic  4.87 us (2%)
    all_to_all x1, waiting for transfers between devices, per_device(): lax.all_to_all(outgoing, ('req', 'grp'), split_axis=0, concat_axis=0, til...  68.2 us
    reduce_scatter x1, waiting for transfers between devices, per_device(): lax.psum_scatter(contract_rows(activated_all, ffn_weight), 'grp', scatter...  58.5 us
    all_gather x1, waiting for transfers between devices, per_device(): lax.all_gather(normed, 'grp', axis=0, tiled=True)  27.8 us
    sub x1, matrix products, normalize(): weights = jnp.where(seen[:, None], jnp.exp(scores - top_score), 0.0)  10.5 us
    dot_general x1, matrix products, contract_rows(): lax.dot_general(activated, weight_block[2], (((1,), (1,)), ((), ())), pre...  8.17 us
    dot_general x1, matrix products, expand_rows(): jnp.dot(rows, weight_block[0], preferred_element_type=jnp.float32)  7.31 us
    all_to_all x1, starting transfers between devices, per_device(): lax.all_to_all(outgoing, ('req', 'grp'), split_axis=0, concat_axis=0, til...  7.3 us
    dot_general x1, matrix products, per_device(): jnp.einsum('rhnk,rke->rnhe', attn_probs, value_rows, preferred_element_ty...  7.14 us
  transfers between devices with their start and end apart: 3, of which 3 were waited for; matrix products, arithmetic and copies ran while one was open for 1% of the time, Pallas kernels for 0%

commit v1 on v0

v1 whole, which is shorter than its diff:
```python
import functools
import math

import jax
import jax.numpy as jnp
from jax import lax
from jax.experimental import pallas as pl
from jax.experimental.pallas import tpu as pltpu
from jax.sharding import PartitionSpec as P

W = 1024
PAGE = 64
HALVES = 2
NT = (((1,), (1,)), ((), ()))
MESH = pl.DeviceIdType.MESH


def layer_kernel(
    lengths_ref, table_ref, arrived_ref, hidden_ref, queries_ref, new_ref, gain_ref, ow_hbm, fw_hbm,
    out_ref,
    ow, fw, kv, att, middle, loc, rem, own_part,
    send_pair, send_fold, send_far, got_pair, got_fold, got_far,
    w_sem, ssem, rsem,
):
    requests, wpages = table_ref.shape
    page = arrived_ref.shape[1]
    pair_width = arrived_ref.shape[2]
    hd = pair_width // 2
    tok, width = queries_ref.shape
    heads = width // hd
    new = tok // requests
    cached = wpages * page
    keys = cached + new
    per_half = requests // HALVES
    rows = tok // HALVES
    ff = fw.shape[2]
    group = 4
    for_heads = 4

    me_r = lax.axis_index("req")
    g = lax.axis_index("grp")
    hi, lo = g // 2, lax.rem(g, 2)
    partner = (me_r, hi * 2 + (1 - lo))
    peer = (me_r, (1 - hi) * 2 + lo)

    ow_copy = pltpu.make_async_copy(ow_hbm, ow, w_sem.at[0])
    ow_copy.start()
    fw_copies = [pltpu.make_async_copy(fw_hbm.at[k], fw.at[k], w_sem.at[k + 1]) for k in range(3)]
    for copy in fw_copies:
        copy.start()

    barrier = pltpu.get_barrier_semaphore()
    for other in (partner, peer):
        pl.semaphore_signal(barrier, inc=1, device_id=other, device_id_type=MESH)
    pl.semaphore_wait(barrier, 2)

    def remote(src, dst, slot, where):
        return pltpu.make_async_remote_copy(
            src_ref=src, dst_ref=dst, send_sem=ssem.at[slot], recv_sem=rsem.at[slot],
            device_id=where, device_id_type=MESH,
        )

    to_partner = [remote(loc.at[c, 0], loc.at[c, 1], c, partner) for c in range(HALVES)]
    to_peer = [remote(loc.at[c, 0], rem.at[c, 0], 2 + c, peer) for c in range(HALVES)]
    forward = [remote(rem.at[c, 0], rem.at[c, 1], 4 + c, partner) for c in range(HALVES)]
    pair_sum = [remote(send_pair.at[c], got_pair.at[c], 6 + c, partner) for c in range(HALVES)]
    fold_sum = [remote(send_fold.at[c], got_fold.at[c], 8 + c, partner) for c in range(HALVES)]
    far_sum = [remote(send_far.at[c], got_far.at[c], 10 + c, peer) for c in range(HALVES)]

    scale = math.log2(math.e) / math.sqrt(hd)

    for c in range(HALVES):

        def attend(t, carry):
            r = c * per_half + t
            for j in range(wpages):
                kv[j * page:(j + 1) * page, :] = arrived_ref[table_ref[r, j]]
            kv[cached:keys, :] = new_ref[pl.ds(pl.multiple_of(r * new, new), new), :]
            length = lengths_ref[r]
            first = jnp.maximum(length - W + 1, 0) // PAGE * page
            col = lax.broadcasted_iota(jnp.int32, (new, keys), 1)
            row = lax.broadcasted_iota(jnp.int32, (new, keys), 0)
            pos = jnp.where(col < cached, col + first, col - cached + length)
            top = jnp.where(col < cached, length - 1, row + length)
            seen = (pos <= top) & (pos > row + length - W)
            bias = jnp.where(seen, 0.0, -1e30).astype(jnp.float32)
            for h0 in range(0, heads, for_heads):
                hs = range(h0, min(h0 + for_heads, heads))
                q = jnp.concatenate(
                    [queries_ref[pl.ds(pl.multiple_of(r * new, new), new), h * hd:(h + 1) * hd] for h in hs], axis=0
                )
                s = lax.dot_general(q, kv[:, :hd], NT, preferred_element_type=jnp.float32)
                s = s.reshape(len(hs), new, keys) * scale + bias[None]
                top_score = jnp.max(s, axis=-1, keepdims=True)
                p = jnp.exp2(s - top_score)
                total = jnp.sum(p, axis=-1, keepdims=True)
                p = p.astype(jnp.bfloat16).reshape(len(hs) * new, keys)
                o = jnp.dot(p, kv[:, hd:], preferred_element_type=jnp.float32)
                o = (o.reshape(len(hs), new, hd) / total).astype(jnp.bfloat16)
                for i, h in enumerate(hs):
                    att[pl.ds(pl.multiple_of(t * new, new), new), h * hd:(h + 1) * hd] = o[i]
            return carry

        lax.fori_loop(0, per_half, attend, 0)
        if c == 0:
            ow_copy.wait()
        projected = jnp.dot(att[...], ow[...], preferred_element_type=jnp.float32)
        mid = (hidden_ref[c * rows:(c + 1) * rows, :].astype(jnp.float32) + projected).astype(jnp.bfloat16)
        middle[c * rows:(c + 1) * rows, :] = mid
        mid_f = mid.astype(jnp.float32)
        rs = lax.rsqrt(jnp.mean(mid_f * mid_f, axis=-1, keepdims=True) + 1e-06)
        loc[c, 0] = (mid_f * rs * gain_ref[...].astype(jnp.float32)).astype(jnp.bfloat16)
        to_peer[c].start()
        to_partner[c].start()

    cols = [(a, min(a + 512, ff)) for a in range(0, ff, 512)]

    def ffn(x):
        parts = []
        for a, b in cols:
            gate = jnp.dot(x, fw[0, :, a:b], preferred_element_type=jnp.float32)
            up = jnp.dot(x, fw[1, :, a:b], preferred_element_type=jnp.float32)
            parts.append((jax.nn.gelu(gate, approximate=True) * up).astype(jnp.bfloat16))
        act = jnp.concatenate(parts, axis=1)
        return lax.dot_general(act, fw[2], NT, preferred_element_type=jnp.float32)

    for copy in fw_copies:
        copy.wait()

    def local(c):
        to_partner[c].wait_recv()
        part = ffn(loc[c].reshape(2 * rows, width))
        own_part[c] = part[:rows]
        send_pair[c] = part[rows:].astype(jnp.bfloat16)
        pair_sum[c].start()

    def far(c):
        forward[c].wait_recv()
        part = ffn(rem[c].reshape(2 * rows, width))
        send_fold[c] = part[rows:].astype(jnp.bfloat16)
        fold_sum[c].start()
        return part[:rows]

    def fold(c, part):
        fold_sum[c].wait_recv()
        send_far[c] = (part + got_fold[c].astype(jnp.float32)).astype(jnp.bfloat16)
        far_sum[c].start()

    def finish(c):
        pair_sum[c].wait_recv()
        own = own_part[c] + middle[c * rows:(c + 1) * rows, :].astype(jnp.float32) + got_pair[c].astype(jnp.float32)
        far_sum[c].wait_recv()
        out_ref[c * rows:(c + 1) * rows, :] = (own + got_far[c].astype(jnp.float32)).astype(jnp.bfloat16)

    local(0)
    to_peer[0].wait_recv()
    forward[0].start()
    local(1)
    part = far(0)
    to_peer[1].wait_recv()
    forward[1].start()
    fold(0, part)
    part = far(1)
    fold(1, part)
    finish(0)
    finish(1)
    for copies in (to_partner, to_peer, forward, pair_sum, fold_sum, far_sum):
        for copy in copies:
            copy.wait_send()


def layer(lengths, table, arrived, hidden, queries, new_cache, gain, out_weight, ffn_weight):
    tok, width = queries.shape
    requests, wpages = table.shape
    page, pair_width = arrived.shape[1:]
    new = tok // requests
    rows = tok // HALVES
    bf, f32 = jnp.bfloat16, jnp.float32
    vm = pl.BlockSpec(memory_space=pltpu.VMEM)
    sm = pl.BlockSpec(memory_space=pltpu.SMEM)
    anyspace = pl.BlockSpec(memory_space=pl.ANY)
    half = (HALVES, rows, width)
    return pl.pallas_call(
        layer_kernel,
        out_shape=jax.ShapeDtypeStruct((tok, width), bf),
        in_specs=[sm, sm, vm, vm, vm, vm, vm, anyspace, anyspace],
        out_specs=vm,
        scratch_shapes=[
            pltpu.VMEM(out_weight.shape, bf),
            pltpu.VMEM(ffn_weight.shape, bf),
            pltpu.VMEM((wpages * page + new, pair_width), bf),
            pltpu.VMEM((rows, width), bf),
            pltpu.VMEM((tok, width), bf),
            pltpu.VMEM((HALVES, 2, rows, width), bf),
            pltpu.VMEM((HALVES, 2, rows, width), bf),
            pltpu.VMEM(half, f32),
        ] + [pltpu.VMEM(half, bf)] * 6 + [
            pltpu.SemaphoreType.DMA((4,)),
            pltpu.SemaphoreType.DMA((12,)),
            pltpu.SemaphoreType.DMA((12,)),
        ],
        compiler_params=pltpu.CompilerParams(
            collective_id=1, has_side_effects=True, vmem_limit_bytes=56 * 2**20
        ),
        name="layer",
    )(lengths, table, arrived, hidden, queries, new_cache, gain.reshape(1, -1), out_weight, ffn_weight)


def per_device(
    hidden,
    queries,
    new_cache,
    cache_pool,
    cache_length,
    page_table,
    send_map,
    out_weight,
    norm_gain,
    ffn_weight,
):
    outgoing = cache_pool[send_map[0]]
    arrived = lax.all_to_all(outgoing, ("req", "grp"), split_axis=0, concat_axis=0, tiled=True)
    return layer(
        cache_length, page_table, arrived, hidden, queries, new_cache, norm_gain, out_weight, ffn_weight
    )


def solution(mesh):
    return jax.shard_map(
        per_device,
        mesh=mesh,
        in_specs=(
            P(("req", "grp"), None),
            P(("req", "grp"), None),
            P(("req", "grp"), None),
            P(("req", "grp"), None, None),
            P(("req", "grp")),
            P(("req", "grp"), None),
            P(("req", "grp"), None),
            P(),
            P(),
            P(None, None, "grp"),
        ),
        out_specs=P(("req", "grp"), None),
        check_vma=False,
    )
```

time: 236 us -> 136 us (0.58)
  waiting for transfers between devices: 155 us -> 70.8 us
  Pallas kernels: 0 us -> 47 us
  matrix products: 43.7 us -> 0 us
  between operations: 13.5 us -> 0.03 us
  other arithmetic: 4.87 us -> 0.67 us
    reduce_scatter x1 -> x0, waiting for transfers between devices: 58.5 us -> none  [per_device(): lax.psum_scatter(contract_rows(activated_all, ffn_weight), 'grp', scatter...]
    pallas_call x0 -> x1, Pallas kernels: none -> 47 us  [layer(): pl.pallas_call(layer_kernel, out_shape=jax.ShapeDtypeStruct((tok, width),...]
    dot_general x5 -> x0, matrix products: 33.2 us -> none  [the longest x1 8.17 us: contract_rows(): lax.dot_general(activated, weight_block[2], (((1,), (1,)), ((), ())), pre...]
    all_gather x1 -> x0, waiting for transfers between devices: 27.8 us -> none  [per_device(): lax.all_gather(normed, 'grp', axis=0, tiled=True)]
    sub x1 -> x0, matrix products: 10.5 us -> none  [normalize(): weights = jnp.where(seen[:, None], jnp.exp(scores - top_score), 0.0)]
    unnamed x14 -> x5, local copies, waits for them, and re-layouts: 0.03 us -> 3.71 us
    convert_element_type x3 -> x0, other arithmetic: 3.56 us -> none  [the longest x1 2.47 us: per_device(): return (middle_f + ffn_sum).astype(jnp.bfloat16)]
    all_to_all x1, waiting for transfers between devices: 68.2 us -> 70.8 us  [per_device(): lax.all_to_all(outgoing, ('req', 'grp'), split_axis=0, concat_axis=0, til...]
  transfers between devices with their start and end apart: 3 -> 1, of which waited for: 3 -> 1; matrix products, arithmetic and copies ran while one was open for 1% -> 0% of each run, Pallas kernels for 0% -> 0%
where the time goes in v1:
time: 136 us
  waiting for transfers between devices  70.8 us (52%)
  Pallas kernels  47 us (35%)
  local copies, waits for them, and re-layouts  10.2 us (7%)
  starting transfers between devices  7.3 us (5%)
    all_to_all x1, waiting for transfers between devices, per_device(): lax.all_to_all(outgoing, ('req', 'grp'), split_axis=0, concat_axis=0, til...  70.8 us
    pallas_call x1, Pallas kernels, layer(): pl.pallas_call(layer_kernel, out_shape=jax.ShapeDtypeStruct((tok, width),...  47 us
    all_to_all x1, starting transfers between devices, per_device(): lax.all_to_all(outgoing, ('req', 'grp'), split_axis=0, concat_axis=0, til...  7.3 us
    gather x1, local copies, waits for them, and re-layouts, per_device(): outgoing = cache_pool[send_map[0]]  5.92 us
    unnamed x5, local copies, waits for them, and re-layouts  3.71 us
  transfers between devices with their start and end apart: 1, of which 1 were waited for; matrix products, arithmetic and copies ran while one was open for 0% of the time, Pallas kernels for 0%

profile of v1, /device:TPU:0, one launch (start us, length us, event | category | flops | bytes accessed | tf_op | source)
XLA Modules:
  0.0 136.1 jit_solution(14424030687673668902)
XLA Ops:
  0.0 0.7 fusion
  0.7 5.9 %gather_fusion = bf16[96,64,256]{2,1,0:T(8,128)(2,1)} fusion(bf16[256,64,256]{2,1,0:T(8,128)(2,1)} %param.13, s32[1024]{0:T(1024)S(1)} %pad_clamp_fusion), kind=kCustom, calls=%fused_computation | custom fusion | bytes 6291840 | tf_op jit(solution)/shard_map/gather | solution.py:221
  6.6 0.0 copy-start.1
  6.6 7.3 %all-to-all-start = ((bf16[96,64,256]{2,1,0:T(8,128)(2,1)}), bf16[96,64,256]{2,1,0:T(8,128)(2,1)S(1)}, u32[]{:S(2)}, u32[]{:S(2)}) async-start(bf16[96,64,256]{2,1,0:T(8,128)(2,1)} %gather_fusion), calls=%async_computation | async-start | bytes 6291456 | tf_op jit(solution)/shard_map/all_to_all | solution.py:222
  13.9 0.0 copy-done.1
  13.9 0.6 reshape.31.gain_ref
  14.5 70.8 %all-to-all-done.arrived_ref = bf16[96,64,256]{2,1,0:T(8,128)(2,1)S(1)} async-done(((bf16[96,64,256]{2,1,0:T(8,128)(2,1)}), bf16[96,64,256]{2,1,0:T(8,128)(2,1)S(1)}, u32[]{:S(2)}, u32[]{:S(2)}) %all-to-all-start) | async-done | bytes 3145760 | tf_op jit(solution)/shard_map/all_to_all | solution.py:222
  85.4 0.0 copy-start
  85.4 1.6 %copy-done = bf16[96,64,256]{2,1,0:T(8,128)(2,1)} copy-done((bf16[96,64,256]{2,1,0:T(8,128)(2,1)}, bf16[96,64,256]{2,1,0:T(8,128)(2,1)S(1)}, u32[]{:S(2)}) %copy-start) | copy-done | bytes 3145752
  87.0 47.0 %layer.1 = bf16[256,1536]{1,0:T(8,128)(2,1)} custom-call(s32[4]{0:T(128)} %lengths_ref.1, s32[4,17]{1,0:T(4,128)} %table_ref.1, bf16[96,64,256]{2,1,0:T(8,128)(2,1)} %copy-done, bf16[256,1536]{1,0:T(8,128)(2,1)} %hidden_ref.1, bf16[256,1536]{1,0:T(8,128)(2,1)} %queries_ref.1, bf16[256,256]{1,0:T(8,128)(2,1)} %new_ref.1, bf16[1,1536]{1,0:T(2,128)(2,1)} %reshape.31.gain_ref, ...), custom_call_target="tpu_custom_call" | custom-call | tf_op jit(solution)/shard_map/layer/pallas_call | solution.py:183
  134.0 2.1 %copy.12 = bf16[256,1536]{1,0:T(8,128)(2,1)} copy(bf16[256,1536]{1,0:T(8,128)(2,1)} %layer.1) | data formatting | bytes 1572864
  (1 shorter events, 0.0 us)
Async XLA Ops:
  6.6 7.3 %copy-start.1 = (bf16[1536]{0:T(1024)(128)(2,1)S(1)}, bf16[1536]{0:T(1024)(128)(2,1)}, u32[]{:S(2)}) copy-start(bf16[1536]{0:T(1024)(128)(2,1)} %param.18) | copy-start | bytes 9220
  6.6 78.8 %all-to-all-start = ((bf16[96,64,256]{2,1,0:T(8,128)(2,1)}), bf16[96,64,256]{2,1,0:T(8,128)(2,1)S(1)}, u32[]{:S(2)}, u32[]{:S(2)}) async-start(bf16[96,64,256]{2,1,0:T(8,128)(2,1)} %gather_fusion), calls=%async_computation | async-start | bytes 6291456 | tf_op jit(solution)/shard_map/all_to_all | solution.py:222
  85.4 1.6 %copy-start = (bf16[96,64,256]{2,1,0:T(8,128)(2,1)}, bf16[96,64,256]{2,1,0:T(8,128)(2,1)S(1)}, u32[]{:S(2)}) copy-start(bf16[96,64,256]{2,1,0:T(8,128)(2,1)S(1)} %all-to-all-done.arrived_ref) | copy-start | bytes 9437188

commit v2 on v1

--- a/solution.py
+++ b/solution.py
@@ -34,8 +34,7 @@
     per_half = requests // HALVES
     rows = tok // HALVES
     ff = fw.shape[2]
-    group = 4
-    for_heads = 4
+    for_heads = 6
 
     me_r = lax.axis_index("req")
     g = lax.axis_index("grp")
@@ -60,58 +59,70 @@
             device_id=where, device_id_type=MESH,
         )
 
-    to_partner = [remote(loc.at[c, 0], loc.at[c, 1], c, partner) for c in range(HALVES)]
-    to_peer = [remote(loc.at[c, 0], rem.at[c, 0], 2 + c, peer) for c in range(HALVES)]
-    forward = [remote(rem.at[c, 0], rem.at[c, 1], 4 + c, partner) for c in range(HALVES)]
-    pair_sum = [remote(send_pair.at[c], got_pair.at[c], 6 + c, partner) for c in range(HALVES)]
-    fold_sum = [remote(send_fold.at[c], got_fold.at[c], 8 + c, partner) for c in range(HALVES)]
-    far_sum = [remote(send_far.at[c], got_far.at[c], 10 + c, peer) for c in range(HALVES)]
+    def piece(r, side, where):
+        c, t = r // per_half, lax.rem(r, per_half)
+        at = pl.ds(pl.multiple_of(t * new, new), new)
+        if side == 0:
+            return remote(loc.at[c, 0, at], loc.at[c, 1, at], r, where)
+        return remote(loc.at[c, 0, at], rem.at[c, 0, at], requests + r, where)
+
+    def to_partner(r):
+        return piece(r, 0, partner)
+
+    def to_peer(r):
+        return piece(r, 1, peer)
+
+    base = 2 * requests
+    forward = [remote(rem.at[c, 0], rem.at[c, 1], base + 0 + c, partner) for c in range(HALVES)]
+    pair_sum = [remote(send_pair.at[c], got_pair.at[c], base + 2 + c, partner) for c in range(HALVES)]
+    fold_sum = [remote(send_fold.at[c], got_fold.at[c], base + 4 + c, partner) for c in range(HALVES)]
+    far_sum = [remote(send_far.at[c], got_far.at[c], base + 6 + c, peer) for c in range(HALVES)]
 
     scale = math.log2(math.e) / math.sqrt(hd)
 
-    for c in range(HALVES):
-
-        def attend(t, carry):
-            r = c * per_half + t
-            for j in range(wpages):
-                kv[j * page:(j + 1) * page, :] = arrived_ref[table_ref[r, j]]
-            kv[cached:keys, :] = new_ref[pl.ds(pl.multiple_of(r * new, new), new), :]
-            length = lengths_ref[r]
-            first = jnp.maximum(length - W + 1, 0) // PAGE * page
-            col = lax.broadcasted_iota(jnp.int32, (new, keys), 1)
-            row = lax.broadcasted_iota(jnp.int32, (new, keys), 0)
-            pos = jnp.where(col < cached, col + first, col - cached + length)
-            top = jnp.where(col < cached, length - 1, row + length)
-            seen = (pos <= top) & (pos > row + length - W)
-            bias = jnp.where(seen, 0.0, -1e30).astype(jnp.float32)
-            for h0 in range(0, heads, for_heads):
-                hs = range(h0, min(h0 + for_heads, heads))
-                q = jnp.concatenate(
-                    [queries_ref[pl.ds(pl.multiple_of(r * new, new), new), h * hd:(h + 1) * hd] for h in hs], axis=0
-                )
-                s = lax.dot_general(q, kv[:, :hd], NT, preferred_element_type=jnp.float32)
-                s = s.reshape(len(hs), new, keys) * scale + bias[None]
-                top_score = jnp.max(s, axis=-1, keepdims=True)
-                p = jnp.exp2(s - top_score)
-                total = jnp.sum(p, axis=-1, keepdims=True)
-                p = p.astype(jnp.bfloat16).reshape(len(hs) * new, keys)
-                o = jnp.dot(p, kv[:, hd:], preferred_element_type=jnp.float32)
-                o = (o.reshape(len(hs), new, hd) / total).astype(jnp.bfloat16)
-                for i, h in enumerate(hs):
-                    att[pl.ds(pl.multiple_of(t * new, new), new), h * hd:(h + 1) * hd] = o[i]
-            return carry
-
-        lax.fori_loop(0, per_half, attend, 0)
-        if c == 0:
+    def attend(r, carry):
+        for j in range(wpages):
+            kv[j * page:(j + 1) * page, :] = arrived_ref[table_ref[r, j]]
+        here = pl.ds(pl.multiple_of(r * new, new), new)
+        kv[cached:keys, :] = new_ref[here, :]
+        length = lengths_ref[r]
+        first = jnp.maximum(length - W + 1, 0) // PAGE * page
+        col = lax.broadcasted_iota(jnp.int32, (new, keys), 1)
+        row = lax.broadcasted_iota(jnp.int32, (new, keys), 0)
+        pos = jnp.where(col < cached, col + first, col - cached + length)
+        top = jnp.where(col < cached, length - 1, row + length)
+        seen = (pos <= top) & (pos > row + length - W)
+        bias = jnp.where(seen, 0.0, -1e30).astype(jnp.float32)
+        for h0 in range(0, heads, for_heads):
+            hs = range(h0, min(h0 + for_heads, heads))
+            q = jnp.concatenate([queries_ref[here, h * hd:(h + 1) * hd] for h in hs], axis=0)
+            s = lax.dot_general(q, kv[:, :hd], NT, preferred_element_type=jnp.float32)
+            s = s.reshape(len(hs), new, keys) * scale + bias[None]
+            top_score = jnp.max(s, axis=-1, keepdims=True)
+            p = jnp.exp2(s - top_score)
+            total = jnp.sum(p, axis=-1, keepdims=True)
+            p = p.astype(jnp.bfloat16).reshape(len(hs) * new, keys)
+            o = jnp.dot(p, kv[:, hd:], preferred_element_type=jnp.float32)
+            o = (o.reshape(len(hs), new, hd) / total).astype(jnp.bfloat16)
+            for i, h in enumerate(hs):
+                att[:, h * hd:(h + 1) * hd] = o[i]
+
+        @pl.when(r == 0)
+        def _():
             ow_copy.wait()
+
         projected = jnp.dot(att[...], ow[...], preferred_element_type=jnp.float32)
-        mid = (hidden_ref[c * rows:(c + 1) * rows, :].astype(jnp.float32) + projected).astype(jnp.bfloat16)
-        middle[c * rows:(c + 1) * rows, :] = mid
+        mid = (hidden_ref[here, :].astype(jnp.float32) + projected).astype(jnp.bfloat16)
+        middle[here, :] = mid
         mid_f = mid.astype(jnp.float32)
         rs = lax.rsqrt(jnp.mean(mid_f * mid_f, axis=-1, keepdims=True) + 1e-06)
-        loc[c, 0] = (mid_f * rs * gain_ref[...].astype(jnp.float32)).astype(jnp.bfloat16)
-        to_peer[c].start()
-        to_partner[c].start()
+        normed = (mid_f * rs * gain_ref[...].astype(jnp.float32)).astype(jnp.bfloat16)
+        loc[r // per_half, 0, pl.ds(pl.multiple_of(lax.rem(r, per_half) * new, new), new), :] = normed
+        to_peer(r).start()
+        to_partner(r).start()
+        return carry
+
+    lax.fori_loop(0, requests, attend, 0)
 
     cols = [(a, min(a + 512, ff)) for a in range(0, ff, 512)]
 
@@ -128,7 +139,8 @@
         copy.wait()
 
     def local(c):
-        to_partner[c].wait_recv()
+        for t in range(per_half):
+            to_partner(c * per_half + t).wait_recv()
         part = ffn(loc[c].reshape(2 * rows, width))
         own_part[c] = part[:rows]
         send_pair[c] = part[rows:].astype(jnp.bfloat16)
@@ -152,19 +164,25 @@
         far_sum[c].wait_recv()
         out_ref[c * rows:(c + 1) * rows, :] = (own + got_far[c].astype(jnp.float32)).astype(jnp.bfloat16)
 
+    def pass_on(c):
+        for t in range(per_half):
+            to_peer(c * per_half + t).wait_recv()
+        forward[c].start()
+
     local(0)
-    to_peer[0].wait_recv()
-    forward[0].start()
+    pass_on(0)
     local(1)
     part = far(0)
-    to_peer[1].wait_recv()
-    forward[1].start()
+    pass_on(1)
     fold(0, part)
     part = far(1)
     fold(1, part)
     finish(0)
     finish(1)
-    for copies in (to_partner, to_peer, forward, pair_sum, fold_sum, far_sum):
+    for r in range(requests):
+        to_partner(r).wait_send()
+        to_peer(r).wait_send()
+    for copies in (forward, pair_sum, fold_sum, far_sum):
         for copy in copies:
             copy.wait_send()
 
@@ -189,15 +207,15 @@
             pltpu.VMEM(out_weight.shape, bf),
             pltpu.VMEM(ffn_weight.shape, bf),
             pltpu.VMEM((wpages * page + new, pair_width), bf),
-            pltpu.VMEM((rows, width), bf),
+            pltpu.VMEM((new, width), bf),
             pltpu.VMEM((tok, width), bf),
             pltpu.VMEM((HALVES, 2, rows, width), bf),
             pltpu.VMEM((HALVES, 2, rows, width), bf),
             pltpu.VMEM(half, f32),
         ] + [pltpu.VMEM(half, bf)] * 6 + [
             pltpu.SemaphoreType.DMA((4,)),
-            pltpu.SemaphoreType.DMA((12,)),
-            pltpu.SemaphoreType.DMA((12,)),
+            pltpu.SemaphoreType.DMA((2 * requests + 4 * HALVES,)),
+            pltpu.SemaphoreType.DMA((2 * requests + 4 * HALVES,)),
         ],
         compiler_params=pltpu.CompilerParams(
             collective_id=1, has_side_effects=True, vmem_limit_bytes=56 * 2**20
@@ -206,7 +224,82 @@
     )(lengths, table, arrived, hidden, queries, new_cache, gain.reshape(1, -1), out_weight, ffn_weight)
 
 
+def exchange_kernel(map_ref, pool_hbm, out_ref, pool, outgoing, pool_sem, ssem, rsem, *, n, groups):
+    cap = map_ref.shape[1] // n
+    me_r = lax.axis_index("req")
+    me_g = lax.axis_index("grp")
+    me = me_r * groups + me_g
+    load = pltpu.make_async_copy(pool_hbm, pool, pool_sem)
+    load.start()
+
+    barrier = pltpu.get_barrier_semaphore()
+
+    def greet(k, carry):
+        other = lax.rem(me + k, n)
+        pl.semaphore_signal(
+            barrier, inc=1, device_id=(other // groups, lax.rem(other, groups)), device_id_type=MESH
+        )
+        return carry
+
+    lax.fori_loop(1, n, greet, 0)
+    load.wait()
+    pl.semaphore_wait(barrier, n - 1)
+
+    def copy_of(k, source, target, held_by):
+        return pltpu.make_async_remote_copy(
+            src_ref=outgoing.at[pl.ds(source * cap, cap)],
+            dst_ref=out_ref.at[pl.ds(target * cap, cap)],
+            send_sem=ssem.at[k], recv_sem=rsem.at[k],
+            device_id=(held_by // groups, lax.rem(held_by, groups)), device_id_type=MESH,
+        )
+
+    def send(i, carry):
+        odd = lax.rem(i, 2)
+        k = n // 2 + (2 * odd - 1) * ((i + 1) // 2)
+        other = lax.rem(me + k, n)
+        for c in range(cap):
+            outgoing[other * cap + c] = pool[map_ref[0, other * cap + c]]
+        copy_of(k, other, me, other).start()
+        return carry
+
+    lax.fori_loop(0, n - 1, send, 0)
+    for c in range(cap):
+        out_ref[me * cap + c] = pool[map_ref[0, me * cap + c]]
+
+    def receive(k, carry):
+        other = lax.rem(me + k, n)
+        source = lax.rem(me + n - k, n)
+        copy_of(k, other, source, other).wait()
+        return carry
+
+    lax.fori_loop(1, n, receive, 0)
+
+
+def exchange(pool, send_map, n, groups):
+    slots = send_map.shape[1]
+    page = pool.shape[1:]
+    return pl.pallas_call(
+        functools.partial(exchange_kernel, n=n, groups=groups),
+        out_shape=jax.ShapeDtypeStruct((slots,) + page, pool.dtype),
+        in_specs=[pl.BlockSpec(memory_space=pltpu.SMEM), pl.BlockSpec(memory_space=pl.ANY)],
+        out_specs=pl.BlockSpec(memory_space=pltpu.VMEM),
+        scratch_shapes=[
+            pltpu.VMEM(pool.shape, pool.dtype),
+            pltpu.VMEM((slots,) + page, pool.dtype),
+            pltpu.SemaphoreType.DMA,
+            pltpu.SemaphoreType.DMA((n,)),
+            pltpu.SemaphoreType.DMA((n,)),
+        ],
+        compiler_params=pltpu.CompilerParams(
+            collective_id=0, has_side_effects=True, vmem_limit_bytes=56 * 2**20
+        ),
+        name="exchange",
+    )(send_map, pool)
+
+
 def per_device(
+    groups,
+    n,
     hidden,
     queries,
     new_cache,
@@ -218,8 +311,7 @@
     norm_gain,
     ffn_weight,
 ):
-    outgoing = cache_pool[send_map[0]]
-    arrived = lax.all_to_all(outgoing, ("req", "grp"), split_axis=0, concat_axis=0, tiled=True)
+    arrived = exchange(cache_pool, send_map, n, groups)
     return layer(
         cache_length, page_table, arrived, hidden, queries, new_cache, norm_gain, out_weight, ffn_weight
     )
@@ -227,7 +319,7 @@
 
 def solution(mesh):
     return jax.shard_map(
-        per_device,
+        functools.partial(per_device, mesh.shape["grp"], mesh.size),
         mesh=mesh,
         in_specs=(
             P(("req", "grp"), None),

time: 136 us -> 132 us (0.971)
  the two profiles are of different devices: /device:TPU:0 before, /device:TPU:17 now
where the time goes in v2:
time: 132 us
  Pallas kernels  129 us (98%)
  local copies, waits for them, and re-layouts  3.35 us (3%)
    pallas_call x1, Pallas kernels, exchange(): pl.pallas_call(functools.partial(exchange_kernel, n=n, groups=groups), ou...  80.7 us
    pallas_call x1, Pallas kernels, layer(): pl.pallas_call(layer_kernel, out_shape=jax.ShapeDtypeStruct((tok, width),...  47.9 us

profile of v2, /device:TPU:17, one launch (start us, length us, event | category | flops | bytes accessed | tf_op | source)
XLA Modules:
  0.0 132.0 jit_solution(588551237327395578)
XLA Ops:
  0.0 1.3 reshape.3.gain_ref
  1.3 80.7 %exchange.1.arrived_ref = bf16[96,64,256]{2,1,0:T(8,128)(2,1)} custom-call(s32[1,96]{1,0:T(1,128)} %map_ref.1, bf16[256,64,256]{2,1,0:T(8,128)(2,1)} %pool_hbm.1), custom_call_target="tpu_custom_call" | custom-call | tf_op jit(solution)/shard_map/exchange/pallas_call | solution.py:281
  82.0 47.9 %layer.1 = bf16[256,1536]{1,0:T(8,128)(2,1)} custom-call(s32[4]{0:T(128)} %lengths_ref.1, s32[4,17]{1,0:T(4,128)} %table_ref.1, bf16[96,64,256]{2,1,0:T(8,128)(2,1)} %exchange.1.arrived_ref, bf16[256,1536]{1,0:T(8,128)(2,1)} %hidden_ref.1, bf16[256,1536]{1,0:T(8,128)(2,1)} %queries_ref.1, bf16[256,256]{1,0:T(8,128)(2,1)} %new_ref.1, ...), custom_call_target="tpu_custom_call" | custom-call | tf_op jit(solution)/shard_map/layer/pallas_call | solution.py:201
  129.9 2.1 %copy.12 = bf16[256,1536]{1,0:T(8,128)(2,1)} copy(bf16[256,1536]{1,0:T(8,128)(2,1)} %layer.1) | data formatting | bytes 1572864
